TPU v7x, 128 devices: a whole 4x4x4 slice. The times are simulated.
128 devices in a mesh: row: 8 (over y_lo, x), col: 16 (over y_hi, z, core).
Axes of the slice: x: 4, y: 4 (y_hi: 2, y_lo: 2; y = y_hi * 2 + y_lo), z: 4, core: 2. Of those that a mesh axis runs over, the one named last changes fastest.
Arguments:
- acts: bfloat16 [4096, 28672], P('col', 'row'), may hold values from -6 to 6
- grads: bfloat16 [4096, 8192], P('row', 'col'), may hold values from -0.19921875 to 0.19921875
- basis_in: bfloat16 [28672, 6144], P('row', 'col'), may hold values from -0.03125 to 0.03125
- basis_out: bfloat16 [8192, 3072], P('col', 'row'), may hold values from -0.0625 to 0.0625
Outputs:
- eigenvalues: float32 [3072, 6144], P('row', 'col')
All inputs are finite; a program needn't handle non-finite values.
Results may differ from a plain program's by a relative error of at most 0.0034.
Values may be sent and summed in bfloat16 or wider, within the bound.
A program may use at most 128 MiB of HBM per device.

v0:
```python
import jax
import jax.numpy as jnp
from jax import lax
from jax.sharding import PartitionSpec as P

LEN = 1024


def per_device(acts, grads, basis_in, basis_out):
    partial_in = jnp.dot(
        lax.all_gather(acts, "col", axis=0, tiled=True),
        basis_in,
        preferred_element_type=jnp.float32,
    )
    proj_in = lax.psum(partial_in, "row").astype(jnp.bfloat16)
    partial_out = jnp.dot(
        lax.all_gather(grads, "row", axis=0, tiled=True),
        basis_out,
        preferred_element_type=jnp.float32,
    )
    proj_out = lax.psum(partial_out, "col").astype(jnp.bfloat16)
    seq_count = proj_out.shape[0] // LEN
    left = proj_out.reshape(seq_count, LEN, proj_out.shape[1])
    right = proj_in.reshape(seq_count, LEN, proj_in.shape[1])
    tile = jnp.einsum("snk,snj->skj", left, right, preferred_element_type=jnp.float32)
    return jnp.mean(tile * tile, axis=0)


def solution(mesh):
    in_specs = (P("col", "row"), P("row", "col"), P("row", "col"), P("col", "row"))
    out_specs = P("row", "col")
    return jax.shard_map(
        per_device, mesh=mesh, in_specs=in_specs, out_specs=out_specs, check_vma=False
    )
```

profile of v0, /device:TPU:0, one launch (start us, length us, event | category | flops | bytes accessed | tf_op | source)
XLA Modules:
  0.0 449.1 jit_solution(3995247112010438970)
XLA Ops:
  6.5 0.0 copy-start
  6.5 0.0 all-gather.3.cloned.1.call-start
  6.5 0.7 all-gather.3.cloned.1.call-update
  7.3 0.0 all-gather.5.cloned.1.call-start
  7.3 0.7 all-gather.5.cloned.1.call-update
  8.0 56.0 %all-gather.3.cloned.1.call-done = bf16[4096,512]{1,0:T(8,128)(2,1)} async-done(((bf16[512,512]{1,0:T(8,128)(2,1)}), bf16[4096,512]{1,0:T(8,128)(2,1)}) %all-gather.3.cloned.1.call-update) | async-done | bytes 4194320 | tf_op jit(solution)/shard_map/all_gather | solution.py:17
  64.1 7.2 %fusion = f32[4096,384]{1,0:T(8,128)} fusion(bf16[4096,512]{1,0:T(8,128)(2,1)} %all-gather.3.cloned.1.call-done, bf16[512,384]{1,0:T(8,128)(2,1)} %param.7), kind=kOutput, calls=%fused_computation.2 | convolution fusion | flops 1610612736 | bytes 10878976 | tf_op jit(solution)/shard_map/dot_general | solution.py:16
  71.3 143.5 %all-reduce.3 = bf16[4096,384]{1,0:T(8,128)(2,1)} all-reduce(f32[4096,384]{1,0:T(8,128)} %fusion), channel_id=1, replica_groups=mesh['row'=8,'col'=16] {'col'}, use_global_device_ids=true, to_apply=%region_0.0 | all-reduce | flops 1572864 | bytes 9437184 | tf_op jit(solution)/shard_map/psum | solution.py:21
  214.8 72.0 %all-gather.5.cloned.1.call-done = bf16[4096,3584]{1,0:T(8,128)(2,1)} async-done(((bf16[256,3584]{1,0:T(8,128)(2,1)}), bf16[4096,3584]{1,0:T(8,128)(2,1)}) %all-gather.5.cloned.1.call-update) | async-done | bytes 29360144 | tf_op jit(solution)/shard_map/all_gather | solution.py:11
  286.8 0.0 copy-done
  286.8 20.9 %fusion.1 = f32[4096,384]{1,0:T(8,128)} fusion(bf16[4096,3584]{1,0:T(8,128)(2,1)} %all-gather.5.cloned.1.call-done, bf16[3584,384]{1,0:T(8,128)(2,1)S(1)} %copy-done), kind=kOutput, calls=%fused_computation.3 | convolution fusion | flops 11274289152 | bytes 38404096 | tf_op jit(solution)/shard_map/dot_general | solution.py:10
  307.7 129.0 %all-reduce.2 = bf16[4096,384]{1,0:T(8,128)(2,1)} all-reduce(f32[4096,384]{1,0:T(8,128)} %fusion.1), channel_id=1, replica_groups=mesh['row'=8,'col'=16] {'row'}, use_global_device_ids=true, to_apply=%region_1.0 | all-reduce | flops 1572864 | bytes 9437184 | tf_op jit(solution)/shard_map/psum | solution.py:15
  436.7 4.7 %multiply_reduce_fusion = f32[384,384]{1,0:T(8,128)S(1)} fusion(bf16[4,1024,384]{2,1,0:T(8,128)(2,1)} %bitcast.8, bf16[4,1024,384]{2,1,0:T(8,128)(2,1)} %bitcast.9), kind=kOutput, calls=%fused_computation | convolution fusion | flops 1208991744 | bytes 6881280 | tf_op jit(solution)/shard_map/snk,snj->skj/dot_general | solution.py:25
  441.4 0.9 broadcast_multiply_fusion
Async XLA Ops:
  6.5 280.2 %copy-start = (bf16[3584,384]{1,0:T(8,128)(2,1)S(1)}, bf16[3584,384]{1,0:T(8,128)(2,1)}, u32[]{:S(2)}) copy-start(bf16[3584,384]{1,0:T(8,128)(2,1)} %param.6) | copy-start | bytes 8257540
  6.5 57.5 %all-gather.3.cloned.1.call-start = ((), (), s32[]{:S(2)}) async-start(), calls=%async_computation | async-start | bytes 4718592 | tf_op jit(solution)/shard_map/all_gather | solution.py:17
  7.3 279.5 %all-gather.5.cloned.1.call-start = ((), (), s32[]{:S(2)}) async-start(), calls=%async_computation.1 | async-start | bytes 31195136 | tf_op jit(solution)/shard_map/all_gather | solution.py:11
Sparse Core Ops, SparseCore 0:
  9.0 55.0 all-gather.2
  66.6 220.1 all-gather.4
where the time goes:
time: 449 us
  blocking collectives  272 us (61%)
  waiting for transfers between devices  129 us (29%)
  matrix products  32.9 us (7%)
  between operations  13.4 us (3%)
    psum x1, blocking collectives, per_device(): proj_out = lax.psum(partial_out, 'col').astype(jnp.bfloat16)  143 us
    psum x1, blocking collectives, per_device(): proj_in = lax.psum(partial_in, 'row').astype(jnp.bfloat16)  129 us
    all_gather x1, waiting for transfers between devices, per_device(): lax.all_gather(acts, 'col', axis=0, tiled=True)  72 us
    all_gather x1, waiting for transfers between devices, per_device(): lax.all_gather(grads, 'row', axis=0, tiled=True)  56 us
    dot_general x1, matrix products, per_device(): jnp.dot(lax.all_gather(acts, 'col', axis=0, tiled=True), basis_in, prefer...  20.9 us
  transfers between devices with their start and end apart: 2, of which 2 were waited for; matrix products, arithmetic and copies ran while one was open for 2% of the time, Pallas kernels for 0%

commit v1 on v0

v1 whole, which is shorter than its diff:
```python
import jax
import jax.numpy as jnp
from jax import lax
from jax.experimental import pallas as pl
from jax.experimental.pallas import tpu as pltpu
from jax.sharding import PartitionSpec as P

BF = jnp.bfloat16
F32 = jnp.float32
MESH = pl.DeviceIdType.MESH
FIRST, REST = (0, 256), (256, 128)


def kernel(
    a, b, g, h, out,
    abuf, bbuf, gbuf, hbuf,
    stg, acc, rx, lst, lrx, pin,
    zst, zacc, zrx, hst, hrx, pout,
    est, erx,
    loc, ss, rs, xs, xr, ls, lr, ps, pr, gs, gr, zs, zr, es, er,
):
    row, col = lax.axis_index("row"), lax.axis_index("col")
    lo, x = row // 4, row % 4
    c, z, hi = col % 2, (col // 2) % 4, col // 8
    p, z0 = z // 2, z % 2
    rows = a.shape[0]
    half = rows // 2
    depth = h.shape[0]
    kb = b.shape[1]

    def dev(x=x, lo=lo, hi=hi, z=z, c=c):
        return (lo * 4 + x, (hi * 4 + z) * 2 + c)

    d_y = dev(hi=1 - hi)
    d_z = dev(z=z + 1 - 2 * z0)
    d_q = dev(z=3 - z)
    d_c = dev(c=1 - c)
    d_l = dev(lo=1 - lo)
    d_d = dev(lo=1 - lo, z=3 - z)
    d_x = [dev(x=(x + r) % 4) for r in (1, 2, 3)]
    d_2 = dev(z=(z + 2) % 4)

    pending = []

    def copy(src, dst, send, recv, to):
        return pltpu.make_async_remote_copy(
            src_ref=src, dst_ref=dst, send_sem=send, recv_sem=recv, device_id=to, device_id_type=MESH
        )

    def send(src, dst, i, to):
        cp = copy(src, dst, ss.at[i], rs.at[i], to)
        cp.start()
        pending.append(cp)

    def got(dst, i):
        copy(dst, dst, ss.at[i], rs.at[i], d_c).wait_recv()

    own = hi * 4 + z0 * 2 + c
    i_y = (1 - hi) * 4 + z0 * 2 + c
    i_z = hi * 4 + (1 - z0) * 2 + c
    i_d = (1 - hi) * 4 + (1 - z0) * 2 + c

    def sib(i):
        return i + 1 - 2 * c

    top, low = pl.ds(0, half), pl.ds(half, half)
    mine = pl.ds(pl.multiple_of(c * depth, depth), depth)
    other = pl.ds(pl.multiple_of((1 - c) * depth, depth), depth)
    l_a = pltpu.make_async_copy(a, abuf.at[own], loc.at[0])
    l_b = pltpu.make_async_copy(b, bbuf.at[p], loc.at[1])
    l_g = pltpu.make_async_copy(g.at[pl.ds(pl.multiple_of(c * rows, rows), rows)], gbuf.at[x, :, mine], loc.at[2])
    l_h = pltpu.make_async_copy(h, hbuf.at[lo, mine], loc.at[3])
    for cp in (l_g, l_a, l_b, l_h):
        cp.start()

    barrier = pltpu.get_barrier_semaphore()
    friends = [d_y, d_z, d_q, d_c, d_l, d_d, d_2] + d_x
    for to in friends:
        pl.semaphore_signal(barrier, inc=1, device_id=to, device_id_type=MESH)
    pl.semaphore_wait(barrier, len(friends))

    send(g.at[pl.ds(pl.multiple_of((1 - c) * rows, rows), rows)], gbuf.at[x, :, mine], 3, d_c)
    send(a.at[top], abuf.at[own, top], 0, d_y)
    send(a.at[low], abuf.at[own, low], 1, d_z)
    send(b.at[:, pl.ds(*FIRST)], bbuf.at[p, :, pl.ds(*FIRST)], 2, d_q)
    send(a, abuf.at[own], 6, d_c)
    send(h, hbuf.at[lo, mine], 4, d_c)
    send(h, hbuf.at[lo, mine], 5, d_l)
    send(a.at[low], abuf.at[own, low], 7, d_y)
    send(a.at[top], abuf.at[own, top], 8, d_z)
    send(b.at[:, pl.ds(*REST)], bbuf.at[p, :, pl.ds(*REST)], 9, d_q)

    l_g.wait()
    got(gbuf.at[x, :, other], 3)
    for r in (1, 2, 3):
        cp = copy(gbuf.at[x], gbuf.at[x], gs.at[r - 1], gr.at[r - 1], d_x[r - 1])
        cp.start()
        pending.append(cp)

    def x_copy(idx, pb, cols, ch):
        to = idx % 4
        rel = (x - to + 4) % 4
        s = (idx // 4, jnp.maximum(rel, 1) - 1, pb, slice(None), pl.ds(*cols))
        return copy(
            stg.at[idx, pb, :, pl.ds(*cols)], rx.at[s], xs.at[idx, ch], xr.at[idx // 4, jnp.maximum(rel, 1) - 1, ch], dev(x=to)
        )

    def block(idx, pb, cols, ch):
        part = jnp.dot(abuf[idx], bbuf[pb, :, pl.ds(*cols)], preferred_element_type=F32)

        @pl.when(idx % 4 == x)
        def _():
            acc[idx // 4, pb, :, pl.ds(*cols)] = part

        @pl.when(idx % 4 != x)
        def _():
            stg[idx, pb, :, pl.ds(*cols)] = part.astype(BF)
            x_copy(idx, pb, cols, ch).start()

    full = (0, kb)
    l_a.wait()
    l_b.wait()
    got(abuf.at[sib(own)], 6)

    @pl.loop(0, 2)
    def _(j):
        block(hi * 4 + z0 * 2 + (c + j) % 2, p, full, 0)

    got(abuf.at[i_y, top], 0)
    send(abuf.at[i_y, top], abuf.at[i_y, top], 10, d_z)
    send(abuf.at[i_y, top], abuf.at[i_y, top], 11, d_c)
    got(abuf.at[i_z, low], 1)
    send(abuf.at[i_z, low], abuf.at[i_z, low], 12, d_y)
    send(abuf.at[i_z, low], abuf.at[i_z, low], 13, d_c)

    l_h.wait()
    got(hbuf.at[1 - lo, mine], 5)
    send(hbuf.at[1 - lo, mine], hbuf.at[1 - lo, mine], 14, d_c)
    got(hbuf.at[lo, other], 4)
    for r in (1, 2, 3):
        src = (x + 4 - r) % 4
        copy(gbuf.at[src], gbuf.at[src], gs.at[r - 1], gr.at[r - 1], d_x[r - 1]).wait_recv()
    got(hbuf.at[1 - lo, other], 14)

    def z_copy(t):
        rel = jnp.maximum((z - t + 4) % 4, 1) - 1
        return copy(zst.at[t], zrx.at[rel], zs.at[t], zr.at[rel], dev(z=t))

    @pl.loop(0, 4)
    def _(t):
        for k in (0, 1):
            part = jnp.dot(gbuf[t], hbuf[k], preferred_element_type=F32)

            @pl.when(t == z)
            def _():
                zacc[k] = part

            @pl.when(t != z)
            def _():
                zst[t, k] = part.astype(zst.dtype)

        @pl.when(t != z)
        def _():
            z_copy(t).start()

    got(abuf.at[i_y, low], 7)
    send(abuf.at[i_y, low], abuf.at[i_y, low], 15, d_c)
    got(abuf.at[i_z, top], 8)
    send(abuf.at[i_z, top], abuf.at[i_z, top], 16, d_c)
    got(abuf.at[sib(i_y), top], 11)
    got(abuf.at[sib(i_z), low], 13)
    got(abuf.at[sib(i_y), low], 15)
    got(abuf.at[sib(i_z), top], 16)

    def near(j):
        k = j // 2
        h_ = jnp.where(k == 1, 1 - hi, hi)
        z_ = jnp.where(k == 2, 1 - z0, z0)
        return h_ * 4 + z_ * 2 + (c + j) % 2

    @pl.loop(2, 6)
    def _(j):
        block(near(j), p, full, 0)

    got(bbuf.at[1 - p, :, pl.ds(*FIRST)], 2)

    @pl.loop(0, 6)
    def _(j):
        block(near(j), 1 - p, FIRST, 1)

    got(abuf.at[i_d, top], 10)
    send(abuf.at[i_d, top], abuf.at[i_d, top], 17, d_c)
    got(abuf.at[i_d, low], 12)
    send(abuf.at[i_d, low], abuf.at[i_d, low], 18, d_c)
    got(bbuf.at[1 - p, :, pl.ds(*REST)], 9)
    got(abuf.at[sib(i_d), top], 17)
    got(abuf.at[sib(i_d), low], 18)

    @pl.loop(0, 2)
    def _(j):
        idx = (1 - hi) * 4 + (1 - z0) * 2 + (c + j) % 2
        block(idx, p, full, 0)
        block(idx, 1 - p, FIRST, 1)
        block(idx, 1 - p, REST, 2)

    @pl.loop(0, 6)
    def _(j):
        block(near(j), 1 - p, REST, 2)

    for r in (1, 2, 3):
        copy(zst.at[0], zrx.at[r - 1], zs.at[0], zr.at[r - 1], d_c).wait_recv()
    for k in (0, 1):
        zacc[k] = zacc[k] + zrx[0, k].astype(F32) + zrx[1, k].astype(F32) + zrx[2, k].astype(F32)
        hst[k] = zacc[k].astype(hst.dtype)
    send(hst, hrx, 19, d_y)

    pieces = ((p, full), (1 - p, FIRST), (1 - p, REST))
    for ch, (pb, cols) in enumerate(pieces):
        cs = pl.ds(*cols)
        for k, hh in enumerate((1 - lo, lo)):
            for r in range(3):
                ref = rx.at[hh, r, pb, :, cs]
                copy(ref, ref, xs.at[0, ch], xr.at[hh, r, ch], d_c).wait_recv()
            total = acc[hh, pb, :, cs]
            for r in range(3):
                total = total + rx[hh, r, pb, :, cs].astype(F32)
            if k == 0:
                lst[pb, :, cs] = total.astype(lst.dtype)
                cp = copy(lst.at[pb, :, cs], lrx.at[pb, :, cs], ls.at[ch], lr.at[ch], d_l)
                cp.start()
                pending.append(cp)
            else:
                acc[hh, pb, :, cs] = total

    got(hrx, 19)
    at = pl.ds(pl.multiple_of((z0 * 2 + c) * rows, rows), rows)
    at_c = pl.ds(pl.multiple_of((z0 * 2 + 1 - c) * rows, rows), rows)
    at_z = pl.ds(pl.multiple_of(((1 - z0) * 2 + c) * rows, rows), rows)
    at_d = pl.ds(pl.multiple_of(((1 - z0) * 2 + 1 - c) * rows, rows), rows)
    for k in (0, 1):
        pout[k, at] = (zacc[k] + hrx[k].astype(F32)).astype(BF)
    send(pout.at[:, at], pout.at[:, at], 20, d_z)
    send(pout.at[:, at], pout.at[:, at], 21, d_c)

    here = pl.ds(pl.multiple_of(x * rows, rows), rows)
    for ch, (pb, cols) in enumerate(pieces):
        cs = pl.ds(*cols)
        ref = lrx.at[pb, :, cs]
        copy(ref, ref, ls.at[ch], lr.at[ch], d_l).wait_recv()
        pin[pb, here, cs] = (acc[lo, pb, :, cs] + lrx[pb, :, cs].astype(F32)).astype(BF)
        for r in (1, 2, 3):
            ref = pin.at[pb, here, cs]
            cp = copy(ref, ref, ps.at[ch, r - 1], pr.at[ch, r - 1], d_x[r - 1])
            cp.start()
            pending.append(cp)

    got(pout.at[:, at_z], 20)
    send(pout.at[:, at_z], pout.at[:, at_z], 22, d_c)
    got(pout.at[:, at_c], 21)
    got(pout.at[:, at_d], 22)
    for ch, (pb, cols) in enumerate(pieces):
        for r in (1, 2, 3):
            src = pl.ds(pl.multiple_of((x + 4 - r) % 4 * rows, rows), rows)
            ref = pin.at[pb, src, pl.ds(*cols)]
            copy(ref, ref, ps.at[ch, r - 1], pr.at[ch, r - 1], d_c).wait_recv()

    def squares(k, pb):
        t = lax.dot_general(pout[k], pin[pb], (((0,), (0,)), ((), ())), preferred_element_type=F32)
        return t * t

    for i, (k, pb, to) in enumerate(((1 - lo, 1 - p, d_d), (1 - lo, p, d_l), (lo, 1 - p, d_q))):
        est[i] = squares(k, pb).astype(est.dtype)
        cp = copy(est.at[i], erx.at[i], es.at[i], er.at[i], to)
        cp.start()
        pending.append(cp)
    total = squares(lo, p)
    for i in range(3):
        copy(erx.at[i], erx.at[i], es.at[i], er.at[i], d_c).wait_recv()
        total = total + erx[i].astype(F32)
    out[...] = total * 0.25

    for cp in pending:
        cp.wait_send()

    @pl.loop(0, 8)
    def _(idx):
        @pl.when(idx % 4 != x)
        def _():
            for ch, (pb, cols) in enumerate(pieces):
                x_copy(idx, pb, cols, ch).wait_send()

    @pl.loop(0, 4)
    def _(t):
        @pl.when(t != z)
        def _():
            z_copy(t).wait_send()


def per_device(acts, grads, basis_in, basis_out):
    rows, feats = acts.shape
    kb = basis_in.shape[1]
    depth, kg = basis_out.shape
    dma = pltpu.SemaphoreType.DMA
    return pl.pallas_call(
        kernel,
        out_shape=jax.ShapeDtypeStruct((kg, kb), F32),
        in_specs=[pl.BlockSpec(memory_space=pl.ANY)] * 4,
        out_specs=pl.BlockSpec(memory_space=pltpu.VMEM),
        scratch_shapes=[
            pltpu.VMEM((8, rows, feats), BF),
            pltpu.VMEM((2, feats, kb), BF),
            pltpu.VMEM((4, rows, 2 * depth), BF),
            pltpu.VMEM((2, 2 * depth, kg), BF),
            pltpu.VMEM((8, 2, rows, kb), BF),
            pltpu.VMEM((2, 2, rows, kb), F32),
            pltpu.VMEM((2, 3, 2, rows, kb), BF),
            pltpu.VMEM((2, rows, kb), BF),
            pltpu.VMEM((2, rows, kb), BF),
            pltpu.VMEM((2, 4 * rows, kb), BF),
            pltpu.VMEM((4, 2, rows, kg), BF),
            pltpu.VMEM((2, rows, kg), F32),
            pltpu.VMEM((3, 2, rows, kg), BF),
            pltpu.VMEM((2, rows, kg), F32),
            pltpu.VMEM((2, rows, kg), F32),
            pltpu.VMEM((2, 4 * rows, kg), BF),
            pltpu.VMEM((3, kg, kb), BF),
            pltpu.VMEM((3, kg, kb), BF),
            dma((4,)),
            dma((23,)), dma((23,)),
            dma((8, 3)), dma((2, 3, 3)),
            dma((3,)), dma((3,)),
            dma((3, 3)), dma((3, 3)),
            dma((3,)), dma((3,)),
            dma((4,)), dma((3,)),
            dma((3,)), dma((3,)),
        ],
        compiler_params=pltpu.CompilerParams(
            collective_id=0, has_side_effects=True, vmem_limit_bytes=58 * 2**20
        ),
        cost_estimate=pl.CostEstimate(flops=14 * 10**9, bytes_accessed=7 * 10**6, transcendentals=0),
    )(acts, basis_in, grads, basis_out)


def solution(mesh):
    in_specs = (P("col", "row"), P("row", "col"), P("row", "col"), P("col", "row"))
    return jax.shard_map(
        per_device, mesh=mesh, in_specs=in_specs, out_specs=P("row", "col"), check_vma=False
    )
```

time: 449 us -> 152 us (0.34)
  blocking collectives: 272 us -> 0 us
  Pallas kernels: 0 us -> 149 us
  waiting for transfers between devices: 129 us -> 0 us
  matrix products: 32.9 us -> 0 us
  between operations: 13.4 us -> 0.01 us
    psum x2 -> x0, blocking collectives: 272 us -> none  [the longest x1 143 us: per_device(): proj_out = lax.psum(partial_out, 'col').astype(jnp.bfloat16)]
    pallas_call x0 -> x1, Pallas kernels: none -> 149 us  [per_device(): pl.pallas_call(kernel, out_shape=jax.ShapeDtypeStruct((kg, kb), F32), in_...]
    all_gather x2 -> x0, waiting for transfers between devices: 128 us -> none  [the longest x1 72 us: per_device(): lax.all_gather(acts, 'col', axis=0, tiled=True)]
    dot_general x3 -> x0, matrix products: 32.9 us -> none  [the longest x1 20.9 us: per_device(): jnp.dot(lax.all_gather(acts, 'col', axis=0, tiled=True), basis_in, prefer...]
  transfers between devices with their start and end apart: 2 -> 0, of which waited for: 2 -> 0; matrix products, arithmetic and copies ran while one was open for 2% -> 0% of each run, Pallas kernels for 0% -> 0%
where the time goes in v1:
time: 152 us; the launch traced here: 151 us
  Pallas kernels  149 us (98%)
  local copies, waits for them, and re-layouts  1.92 us (1%)
    pallas_call x1, Pallas kernels, per_device(): pl.pallas_call(kernel, out_shape=jax.ShapeDtypeStruct((kg, kb), F32), in_...  149 us

profile of v1, /device:TPU:0, one launch (start us, length us, event | category | flops | bytes accessed | tf_op | source)
XLA Modules:
  0.0 151.1 jit_solution(12313743574470613715)
XLA Ops:
  0.0 149.2 %shard_map.46 = f32[384,384]{1,0:T(8,128)} custom-call(bf16[256,3584]{1,0:T(8,128)(2,1)} %a.1, bf16[3584,384]{1,0:T(8,128)(2,1)} %b.1, bf16[512,512]{1,0:T(8,128)(2,1)} %g.1, bf16[512,384]{1,0:T(8,128)(2,1)} %h.1), custom_call_target="tpu_custom_call" | custom-call | flops 14000000000 | bytes 7000000 | tf_op jit(solution)/shard_map/pallas_call | solution.py:304
  149.2 1.9 %copy.6 = f32[384,384]{1,0:T(8,128)} copy(f32[384,384]{1,0:T(8,128)} %shard_map.46) | data formatting | bytes 1179648

commit v2 on v0

v2 whole, which is shorter than its diff:
```python
import jax
import jax.numpy as jnp
from jax import lax
from jax.experimental import pallas as pl
from jax.experimental.pallas import tpu as pltpu
from jax.sharding import PartitionSpec as P

BF = jnp.bfloat16
F32 = jnp.float32
MESH = pl.DeviceIdType.MESH
FIRST, REST = (0, 256), (256, 128)


def kernel(
    a, b, g, h, out,
    abuf, bbuf, gbuf, hbuf,
    cf, stg, acc, rx, lst, lrx, pin,
    zst, zacc, zrx, hst, hrx, pout,
    est, erx,
    loc, ss, rs, xs, xr, ls, lr, ps, pr, gs, gr, zs, zr, es, er,
):
    row, col = lax.axis_index("row"), lax.axis_index("col")
    lo, x = row // 4, row % 4
    c, z, hi = col % 2, (col // 2) % 4, col // 8
    p, z0 = z // 2, z % 2
    rows, feats = a.shape
    half = rows // 2
    part_rows = rows // 4
    depth, kg = h.shape
    kb = b.shape[1]

    def dev(x=x, lo=lo, hi=hi, z=z, c=c):
        return (lo * 4 + x, (hi * 4 + z) * 2 + c)

    d_y = dev(hi=1 - hi)
    d_z = dev(z=z + 1 - 2 * z0)
    d_q = dev(z=3 - z)
    d_c = dev(c=1 - c)
    d_l = dev(lo=1 - lo)
    d_d = dev(lo=1 - lo, z=3 - z)
    d_x = [dev(x=(x + r) % 4) for r in (1, 2, 3)]
    d_2 = dev(z=(z + 2) % 4)

    pending = []

    def copy(src, dst, send, recv, to):
        return pltpu.make_async_remote_copy(
            src_ref=src, dst_ref=dst, send_sem=send, recv_sem=recv, device_id=to, device_id_type=MESH
        )

    def start(cp):
        cp.start()
        pending.append(cp)

    def send(src, dst, i, to):
        start(copy(src, dst, ss.at[i], rs.at[i], to))

    def got(dst, i):
        copy(dst, dst, ss.at[i], rs.at[i], d_c).wait_recv()

    s_o = hi * 2 + z0
    s_y = (1 - hi) * 2 + z0
    s_z = hi * 2 + 1 - z0
    s_d = (1 - hi) * 2 + 1 - z0
    top, low = pl.ds(0, half), pl.ds(half, half)
    mine = pl.ds(pl.multiple_of(c * depth, depth), depth)
    other = pl.ds(pl.multiple_of((1 - c) * depth, depth), depth)
    l_a = [pltpu.make_async_copy(a.at[pl.ds(k * half, half)], abuf.at[s_o, k, c], loc.at[k]) for k in (0, 1)]
    l_b = pltpu.make_async_copy(b, bbuf.at[p], loc.at[2])
    l_g = pltpu.make_async_copy(g.at[pl.ds(pl.multiple_of(c * rows, rows), rows)], gbuf.at[x, :, mine], loc.at[3])
    l_h = pltpu.make_async_copy(h, hbuf.at[lo, mine], loc.at[4])
    for cp in (l_g, l_h, *l_a, l_b):
        cp.start()

    barrier = pltpu.get_barrier_semaphore()
    friends = [d_y, d_z, d_q, d_c, d_l, d_d, d_2] + d_x
    for to in friends:
        pl.semaphore_signal(barrier, inc=1, device_id=to, device_id_type=MESH)
    pl.semaphore_wait(barrier, len(friends))

    send(g.at[pl.ds(pl.multiple_of((1 - c) * rows, rows), rows)], gbuf.at[x, :, mine], 0, d_c)
    send(h, hbuf.at[lo, mine], 1, d_l)
    send(a.at[top], abuf.at[s_o, 0, c], 2, d_y)
    send(a.at[low], abuf.at[s_o, 1, c], 3, d_z)
    send(b.at[:, pl.ds(*FIRST)], bbuf.at[p, :, pl.ds(*FIRST)], 4, d_q)
    send(a.at[top], abuf.at[s_o, 0, c], 5, d_c)
    send(a.at[low], abuf.at[s_o, 1, c], 6, d_c)
    send(h, hbuf.at[lo, mine], 7, d_c)
    send(a.at[low], abuf.at[s_o, 1, c], 8, d_y)
    send(a.at[top], abuf.at[s_o, 0, c], 9, d_z)
    send(b.at[:, pl.ds(*REST)], bbuf.at[p, :, pl.ds(*REST)], 10, d_q)

    l_g.wait()
    got(gbuf.at[x, :, other], 0)
    for r in (1, 2, 3):
        start(copy(gbuf.at[x], gbuf.at[x], gs.at[r - 1], gr.at[r - 1], d_x[r - 1]))

    def x_copy(s, k, pb, cols, ch, r):
        cs = pl.ds(*cols)
        quarter = pl.ds(pl.multiple_of((x + r) % 4 * part_rows, part_rows), part_rows)
        u = s * 2 + k
        return copy(
            stg.at[s, k, pb, quarter, cs], rx.at[r - 1, s, k, pb, :, cs], xs.at[u, ch, r - 1], xr.at[u, ch, r - 1], d_x[r - 1]
        )

    full = (0, kb)
    kept = pl.ds(pl.multiple_of(x * part_rows, part_rows), part_rows)

    def block(s, k, pb, cols, chunks):
        cs = pl.ds(*cols)
        lhs = abuf[s, k].reshape(rows, feats)
        part = jnp.dot(lhs, bbuf[pb, :, cs], preferred_element_type=F32)
        cf[:, cs] = part
        stg[s, k, pb, :, cs] = part.astype(BF)
        for ch, piece in chunks:
            for r in (1, 2, 3):
                x_copy(s, k, pb, piece, ch, r).start()
        acc[s, k, pb, :, cs] = cf[kept, cs]

    def first(s, k):
        block(s, k, p, full, [(0, full)])

    for cp in l_a:
        cp.wait()
    l_b.wait()
    got(abuf.at[s_o, 0, 1 - c], 5)
    got(abuf.at[s_o, 1, 1 - c], 6)

    @pl.loop(0, 2)
    def _(k):
        first(s_o, k)

    got(abuf.at[s_y, 0, c], 2)
    send(abuf.at[s_y, 0, c], abuf.at[s_y, 0, c], 11, d_c)
    got(abuf.at[s_z, 1, c], 3)
    send(abuf.at[s_z, 1, c], abuf.at[s_z, 1, c], 12, d_c)
    got(hbuf.at[1 - lo, mine], 1)
    send(hbuf.at[1 - lo, mine], hbuf.at[1 - lo, mine], 13, d_c)
    got(abuf.at[s_y, 0, 1 - c], 11)
    got(abuf.at[s_z, 1, 1 - c], 12)

    @pl.loop(0, 2)
    def _(k):
        first(jnp.where(k == 0, s_y, s_z), k)

    l_h.wait()
    got(hbuf.at[lo, other], 7)
    got(hbuf.at[1 - lo, other], 13)
    for r in (1, 2, 3):
        src = (x + 4 - r) % 4
        copy(gbuf.at[src], gbuf.at[src], gs.at[r - 1], gr.at[r - 1], d_c).wait_recv()

    def z_copy(t):
        rel = jnp.maximum((z - t + 4) % 4, 1) - 1
        return copy(zst.at[t], zrx.at[rel], zs.at[t], zr.at[rel], dev(z=t))

    @pl.loop(0, 4)
    def _(t):
        for k in (0, 1):
            part = jnp.dot(gbuf[t], hbuf[k], preferred_element_type=F32)

            @pl.when(t == z)
            def _():
                zacc[k] = part

            @pl.when(t != z)
            def _():
                zst[t, k] = part.astype(zst.dtype)

        @pl.when(t != z)
        def _():
            z_copy(t).start()

    got(abuf.at[s_y, 1, c], 8)
    send(abuf.at[s_z, 1, c], abuf.at[s_z, 1, c], 15, d_y)
    send(abuf.at[s_y, 1, c], abuf.at[s_y, 1, c], 16, d_c)
    got(abuf.at[s_z, 0, c], 9)
    send(abuf.at[s_y, 0, c], abuf.at[s_y, 0, c], 14, d_z)
    send(abuf.at[s_z, 0, c], abuf.at[s_z, 0, c], 17, d_c)
    got(abuf.at[s_y, 1, 1 - c], 16)
    got(abuf.at[s_z, 0, 1 - c], 17)

    @pl.loop(0, 2)
    def _(k):
        first(jnp.where(k == 0, s_z, s_y), k)

    got(bbuf.at[1 - p, :, pl.ds(*FIRST)], 4)

    def near(j):
        return jnp.where(j < 2, s_o, jnp.where(j < 4, s_y, s_z))

    @pl.loop(0, 6)
    def _(j):
        block(near(j), j % 2, 1 - p, FIRST, [(1, FIRST)])

    def add_x(zz, pb, cols, chunks, i):
        cs = pl.ds(*cols)
        for hh in (1 - lo, lo):
            s = hh * 2 + zz
            for k in (0, 1):
                for ch, piece in chunks:
                    for r in range(3):
                        ref = rx.at[r, s, k, pb, :, pl.ds(*piece)]
                        copy(ref, ref, xs.at[0, 0, 0], xr.at[s * 2 + k, ch, r], d_c).wait_recv()
            total = acc[s, :, pb, :, cs]
            for r in range(3):
                total = total + rx[r, s, :, pb, :, cs].astype(F32)
            if hh is lo:
                acc[s, :, pb, :, cs] = total
            else:
                lst[zz, :, pb, :, cs] = total.astype(lst.dtype)
                start(copy(lst.at[zz, :, pb, :, cs], lrx.at[zz, :, pb, :, cs], ls.at[i], lr.at[i], d_l))

    def add_y(zz, pb, cols, i):
        cs = pl.ds(*cols)
        ref = lrx.at[zz, :, pb, :, cs]
        copy(ref, ref, ls.at[i], lr.at[i], d_c).wait_recv()
        pin[pb, zz, :, x, :, cs] = (acc[lo * 2 + zz, :, pb, :, cs] + lrx[zz, :, pb, :, cs].astype(F32)).astype(BF)
        for r in (1, 2, 3):
            ref = pin.at[pb, zz, :, x, :, cs]
            start(copy(ref, ref, ps.at[i, r - 1], pr.at[i, r - 1], d_x[r - 1]))

    def gathered(zz, pb, cols, i):
        for r in (1, 2, 3):
            ref = pin.at[pb, zz, :, (x + 4 - r) % 4, :, pl.ds(*cols)]
            copy(ref, ref, ps.at[i, r - 1], pr.at[i, r - 1], d_c).wait_recv()

    add_x(z0, p, full, [(0, full)], 0)
    add_x(z0, 1 - p, FIRST, [(1, FIRST)], 1)

    got(bbuf.at[1 - p, :, pl.ds(*REST)], 10)

    @pl.loop(0, 6)
    def _(j):
        block(near(j), j % 2, 1 - p, REST, [(2, REST)])

    for r in (1, 2, 3):
        copy(zst.at[0], zrx.at[r - 1], zs.at[0], zr.at[r - 1], d_c).wait_recv()
    for k in (0, 1):
        zacc[k] = zacc[k] + zrx[0, k].astype(F32) + zrx[1, k].astype(F32) + zrx[2, k].astype(F32)
        hst[k] = zacc[k].astype(hst.dtype)
    send(hst, hrx, 18, d_y)

    add_y(z0, p, full, 0)
    add_y(z0, 1 - p, FIRST, 1)

    got(abuf.at[s_d, 0, c], 14)
    send(abuf.at[s_d, 0, c], abuf.at[s_d, 0, c], 19, d_c)
    got(abuf.at[s_d, 1, c], 15)
    send(abuf.at[s_d, 1, c], abuf.at[s_d, 1, c], 20, d_c)
    got(abuf.at[s_d, 0, 1 - c], 19)
    got(abuf.at[s_d, 1, 1 - c], 20)

    @pl.loop(0, 2)
    def _(k):
        first(s_d, k)

    @pl.loop(0, 2)
    def _(k):
        block(s_d, k, 1 - p, full, [(1, FIRST), (2, REST)])

    add_x(1 - z0, p, full, [(0, full)], 2)
    add_x(z0, 1 - p, REST, [(2, REST)], 3)
    add_x(1 - z0, 1 - p, full, [(1, FIRST), (2, REST)], 4)
    add_y(1 - z0, p, full, 2)
    add_y(z0, 1 - p, REST, 3)
    add_y(1 - z0, 1 - p, full, 4)

    got(hrx, 18)
    for k in (0, 1):
        pout[k, z0, :, c] = (zacc[k] + hrx[k].astype(F32)).astype(BF).reshape(2, half, kg)
    send(pout.at[:, z0, :, c], pout.at[:, z0, :, c], 21, d_z)
    send(pout.at[:, z0, :, c], pout.at[:, z0, :, c], 22, d_c)
    got(pout.at[:, 1 - z0, :, c], 21)
    send(pout.at[:, 1 - z0, :, c], pout.at[:, 1 - z0, :, c], 23, d_c)
    got(pout.at[:, z0, :, 1 - c], 22)
    got(pout.at[:, 1 - z0, :, 1 - c], 23)

    def squares(k, pb):
        left = pout[k].reshape(4 * rows, kg)
        right = pin[pb].reshape(4 * rows, kb)
        t = lax.dot_general(left, right, (((0,), (0,)), ((), ())), preferred_element_type=F32)
        return t * t

    def give(i, k, pb, to):
        est[i] = squares(k, pb).astype(est.dtype)
        start(copy(est.at[i], erx.at[i], es.at[i], er.at[i], to))

    gathered(z0, p, full, 0)
    gathered(1 - z0, p, full, 2)
    give(0, 1 - lo, p, d_l)
    gathered(z0, 1 - p, FIRST, 1)
    gathered(z0, 1 - p, REST, 3)
    gathered(1 - z0, 1 - p, full, 4)
    give(1, 1 - lo, 1 - p, d_d)
    give(2, lo, 1 - p, d_q)
    total = squares(lo, p)
    for i in range(3):
        copy(erx.at[i], erx.at[i], es.at[i], er.at[i], d_c).wait_recv()
        total = total + erx[i].astype(F32)
    out[...] = total * 0.25

    for cp in pending:
        cp.wait_send()

    @pl.loop(0, 8)
    def _(u):
        for ch, (pb, piece) in enumerate(((p, full), (1 - p, FIRST), (1 - p, REST))):
            for r in (1, 2, 3):
                x_copy(u // 2, u % 2, pb, piece, ch, r).wait_send()

    @pl.loop(0, 4)
    def _(t):
        @pl.when(t != z)
        def _():
            z_copy(t).wait_send()


def per_device(acts, grads, basis_in, basis_out):
    rows, feats = acts.shape
    kb = basis_in.shape[1]
    depth, kg = basis_out.shape
    dma = pltpu.SemaphoreType.DMA
    return pl.pallas_call(
        kernel,
        out_shape=jax.ShapeDtypeStruct((kg, kb), F32),
        in_specs=[pl.BlockSpec(memory_space=pl.ANY)] * 4,
        out_specs=pl.BlockSpec(memory_space=pltpu.VMEM),
        scratch_shapes=[
            pltpu.VMEM((4, 2, 2, rows // 2, feats), BF),
            pltpu.VMEM((2, feats, kb), BF),
            pltpu.VMEM((4, rows, 2 * depth), BF),
            pltpu.VMEM((2, 2 * depth, kg), BF),
            pltpu.VMEM((rows, kb), F32),
            pltpu.VMEM((4, 2, 2, rows, kb), BF),
            pltpu.VMEM((4, 2, 2, rows // 4, kb), F32),
            pltpu.VMEM((3, 4, 2, 2, rows // 4, kb), BF),
            pltpu.VMEM((2, 2, 2, rows // 4, kb), BF),
            pltpu.VMEM((2, 2, 2, rows // 4, kb), BF),
            pltpu.VMEM((2, 2, 2, 4, rows // 4, kb), BF),
            pltpu.VMEM((4, 2, rows, kg), BF),
            pltpu.VMEM((2, rows, kg), F32),
            pltpu.VMEM((3, 2, rows, kg), BF),
            pltpu.VMEM((2, rows, kg), F32),
            pltpu.VMEM((2, rows, kg), F32),
            pltpu.VMEM((2, 2, 2, 2, rows // 2, kg), BF),
            pltpu.VMEM((3, kg, kb), BF),
            pltpu.VMEM((3, kg, kb), BF),
            dma((5,)),
            dma((24,)), dma((24,)),
            dma((8, 3, 3)), dma((8, 3, 3)),
            dma((5,)), dma((5,)),
            dma((5, 3)), dma((5, 3)),
            dma((3,)), dma((3,)),
            dma((4,)), dma((3,)),
            dma((3,)), dma((3,)),
        ],
        compiler_params=pltpu.CompilerParams(
            collective_id=0, has_side_effects=True, vmem_limit_bytes=58 * 2**20
        ),
        cost_estimate=pl.CostEstimate(flops=14 * 10**9, bytes_accessed=7 * 10**6, transcendentals=0),
    )(acts, basis_in, grads, basis_out)


def solution(mesh):
    in_specs = (P("col", "row"), P("row", "col"), P("row", "col"), P("col", "row"))
    return jax.shard_map(
        per_device, mesh=mesh, in_specs=in_specs, out_specs=P("row", "col"), check_vma=False
    )
```

time: 449 us -> 138 us (0.31)
  blocking collectives: 272 us -> 0 us
  Pallas kernels: 0 us -> 135 us
  waiting for transfers between devices: 129 us -> 0 us
  matrix products: 32.9 us -> 0 us
  between operations: 13.4 us -> 0.01 us
    psum x2 -> x0, blocking collectives: 272 us -> none  [the longest x1 143 us: per_device(): proj_out = lax.psum(partial_out, 'col').astype(jnp.bfloat16)]
    pallas_call x0 -> x1, Pallas kernels: none -> 135 us  [per_device(): pl.pallas_call(kernel, out_shape=jax.ShapeDtypeStruct((kg, kb), F32), in_...]
    all_gather x2 -> x0, waiting for transfers between devices: 128 us -> none  [the longest x1 72 us: per_device(): lax.all_gather(acts, 'col', axis=0, tiled=True)]
    dot_general x3 -> x0, matrix products: 32.9 us -> none  [the longest x1 20.9 us: per_device(): jnp.dot(lax.all_gather(acts, 'col', axis=0, tiled=True), basis_in, prefer...]
  transfers between devices with their start and end apart: 2 -> 0, of which waited for: 2 -> 0; matrix products, arithmetic and copies ran while one was open for 2% -> 0% of each run, Pallas kernels for 0% -> 0%
where the time goes in v2:
time: 138 us; the launch traced here: 136 us
  Pallas kernels  135 us (98%)
  local copies, waits for them, and re-layouts  1.92 us (1%)
    pallas_call x1, Pallas kernels, per_device(): pl.pallas_call(kernel, out_shape=jax.ShapeDtypeStruct((kg, kb), F32), in_...  135 us

profile of v2, /device:TPU:0, one launch (start us, length us, event | category | flops | bytes accessed | tf_op | source)
XLA Modules:
  0.0 136.5 jit_solution(16996361995773195627)
XLA Ops:
  0.0 134.6 %shard_map.46 = f32[384,384]{1,0:T(8,128)} custom-call(bf16[256,3584]{1,0:T(8,128)(2,1)} %a.1, bf16[3584,384]{1,0:T(8,128)(2,1)} %b.1, bf16[512,512]{1,0:T(8,128)(2,1)} %g.1, bf16[512,384]{1,0:T(8,128)(2,1)} %h.1), custom_call_target="tpu_custom_call" | custom-call | flops 14000000000 | bytes 7000000 | tf_op jit(solution)/shard_map/pallas_call | solution.py:324
  134.6 1.9 %copy.6 = f32[384,384]{1,0:T(8,128)} copy(f32[384,384]{1,0:T(8,128)} %shard_map.46) | data formatting | bytes 1179648

commit v3 on v0

v3 whole, which is shorter than its diff:
```python
import jax
import jax.numpy as jnp
from jax import lax
from jax.experimental import pallas as pl
from jax.experimental.pallas import tpu as pltpu
from jax.sharding import PartitionSpec as P

BF = jnp.bfloat16
F32 = jnp.float32
MESH = pl.DeviceIdType.MESH
OWN, FIRST, REST = (0, 0, 384), (1, 0, 256), (1, 256, 128)
PIECES = (OWN, FIRST, REST)
TOP, LOW, THIRD, FOURTH, ALL = (0, 2), (2, 2), (2, 1), (3, 1), (0, 4)
MESSAGES = {TOP: [TOP], LOW: [THIRD, FOURTH], THIRD: [THIRD], FOURTH: [FOURTH], ALL: [TOP, THIRD, FOURTH]}


def kernel(
    a, b, g, h, out,
    abuf, bbuf, gbuf, hbuf,
    cf, stg, acc, rx, lst, lrx, pin,
    zst, zall, zrx, pout,
    est, erx, esum,
    loc, ss, rs, xs, xr, ls, lr, ps, pr, gs, gr, zs, zr, es, er,
):
    row, col = lax.axis_index("row"), lax.axis_index("col")
    lo, x = row // 4, row % 4
    c, z, hi = col % 2, (col // 2) % 4, col // 8
    z0 = z % 2
    rows, feats = a.shape
    qr = rows // 4
    xrows = 2 * qr // 4
    depth, kg = h.shape
    kb = b.shape[1]

    def dev(x=x, lo=lo, hi=hi, z=z, c=c):
        return (lo * 4 + x, (hi * 4 + z) * 2 + c)

    d_y = dev(hi=1 - hi)
    d_z = dev(z=z + 1 - 2 * z0)
    d_q = dev(z=3 - z)
    d_c = dev(c=1 - c)
    d_yc = dev(hi=1 - hi, c=1 - c)
    d_l = dev(lo=1 - lo)
    d_b = dev(lo=1 - lo, hi=1 - hi)
    d_x = [dev(x=(x + r) % 4) for r in (1, 2, 3)]
    d_zs = [dev(z=(z + r) % 4) for r in (1, 2, 3)]

    pending = []

    def copy(src, dst, send, recv, to):
        return pltpu.make_async_remote_copy(
            src_ref=src, dst_ref=dst, send_sem=send, recv_sem=recv, device_id=to, device_id_type=MESH
        )

    def start(cp):
        cp.start()
        pending.append(cp)

    def send(src, dst, i, to):
        start(copy(src, dst, ss.at[i], rs.at[i], to))

    def pass_on(ref, i, to):
        send(ref, ref, i, to)

    def got(dst, i):
        copy(dst, dst, ss.at[i], rs.at[i], d_c).wait_recv()

    def span(i, n):
        return pl.ds(pl.multiple_of(i * n, n), n)

    s_o = hi * 2 + z0
    s_y = (1 - hi) * 2 + z0
    s_z = hi * 2 + 1 - z0
    s_d = (1 - hi) * 2 + 1 - z0
    here, there = hi * 2 + c, (1 - hi) * 2 + c
    here_c, there_c = hi * 2 + 1 - c, (1 - hi) * 2 + 1 - c
    own_k, other_k = pl.ds(0, kg), pl.ds(kg, kg)

    def h_at(i, k):
        return hbuf.at[span(i, depth), k]

    l_a = [pltpu.make_async_copy(a.at[pl.ds(k * qr, qr)], abuf.at[s_o, k, c], loc.at[k]) for k in range(4)]
    l_b = pltpu.make_async_copy(b, bbuf.at[:, pl.ds(0, kb)], loc.at[4])
    l_g = pltpu.make_async_copy(g.at[span(c * 2 + hi, rows // 2)], gbuf.at[x, :, span(here, depth)], loc.at[5])
    l_h = pltpu.make_async_copy(h, h_at(here, own_k), loc.at[6])
    for cp in (*l_a, l_b, l_g, l_h):
        cp.start()

    barrier = pltpu.get_barrier_semaphore()
    friends = [d_y, d_c, d_yc, d_l, d_b] + d_x + d_zs
    for to in friends:
        pl.semaphore_signal(barrier, inc=1, device_id=to, device_id_type=MESH)
    pl.semaphore_wait(barrier, len(friends))

    def send_g(i, hh, cc, to):
        send(g.at[span(cc * 2 + hh, rows // 2)], gbuf.at[x, :, span(here, depth)], i, to)

    def send_a(k, i, to):
        send(a.at[pl.ds(k * qr, qr)], abuf.at[s_o, k, c], i, to)

    def b_at(piece):
        return bbuf.at[:, pl.ds(kb + piece[1], piece[2])]

    def send_b(piece, i):
        send(b.at[:, pl.ds(piece[1], piece[2])], b_at(piece), i, d_q)

    send_g(0, 1 - hi, c, d_y)
    send_g(1, 1 - hi, 1 - c, d_yc)
    send_a(0, 2, d_y)
    send_a(2, 3, d_z)
    send_b(FIRST, 4)
    send_a(1, 5, d_y)
    send_a(3, 6, d_z)
    for k in range(4):
        send_a(k, 7 + k, d_c)
    send_g(11, hi, 1 - c, d_c)
    send(h, h_at(here, own_k), 14, d_c)
    send_a(2, 15, d_y)
    send_a(0, 16, d_z)
    send_a(3, 17, d_y)
    send_a(1, 18, d_z)
    send(h, h_at(here, other_k), 12, d_l)
    send(h, h_at(here, other_k), 13, d_b)
    send_b(REST, 19)

    def x_copy(s, q, ch, r):
        pb, c0, w = PIECES[ch]
        u, qs, cs = s * 4 + q[0], pl.ds(*q), pl.ds(c0, w)
        return copy(
            stg.at[s, qs, pb, span((x + r) % 4, xrows), cs], rx.at[r - 1, s, qs, pb, :, cs],
            xs.at[u, ch, r - 1], xr.at[u, ch, r - 1], d_x[r - 1],
        )

    def block(s, q, *chunks):
        qs = pl.ds(*q)
        c0 = PIECES[chunks[0]][0] * kb + PIECES[chunks[0]][1]
        w = sum(PIECES[ch][2] for ch in chunks)
        lhs = abuf[s, qs].reshape(q[1] * 2 * qr, feats)
        part = jnp.dot(lhs, bbuf[:, pl.ds(c0, w)], preferred_element_type=F32)
        for ch in chunks:
            pb, first, width = PIECES[ch]
            cut = part[:, pb * kb + first - c0:][:, :width].reshape(q[1], 2 * qr, width)
            cf[pl.ds(0, q[1]), pb, :, pl.ds(first, width)] = cut
            stg[s, qs, pb, :, pl.ds(first, width)] = cut.astype(BF)
        for ch in chunks:
            for m in MESSAGES[q]:
                for r in (1, 2, 3):
                    x_copy(s, m, ch, r).start()
        for ch in chunks:
            pb, first, width = PIECES[ch]
            cs = pl.ds(first, width)
            acc[s, qs, pb, :, cs] = cf[pl.ds(0, q[1]), pb, span(x, xrows), cs]

    def span_of(chunks):
        return PIECES[chunks[0]][0], pl.ds(PIECES[chunks[0]][1], sum(PIECES[ch][2] for ch in chunks))

    def add_x(i, zz, q, *chunks):
        qs = pl.ds(*q)
        pb, cs = span_of(chunks)
        for hh in (1 - lo, lo):
            s = hh * 2 + zz
            for m in MESSAGES[q]:
                for ch in chunks:
                    for r in range(3):
                        ref = rx.at[r, s, pl.ds(*m), pb, :, pl.ds(*PIECES[ch][1:])]
                        copy(ref, ref, xs.at[0, 0, 0], xr.at[s * 4 + m[0], ch, r], d_c).wait_recv()
            total = acc[s, qs, pb, :, cs]
            for r in range(3):
                total = total + rx[r, s, qs, pb, :, cs].astype(F32)
            if hh is lo:
                acc[s, qs, pb, :, cs] = total
            else:
                ref = lst.at[zz, qs, pb, :, cs]
                ref[...] = total.astype(lst.dtype)
                start(copy(ref, lrx.at[zz, qs, pb, :, cs], ls.at[i], lr.at[i], d_l))

    def add_y(i, zz, q, *chunks):
        qs = pl.ds(*q)
        pb, cs = span_of(chunks)
        ref = lrx.at[zz, qs, pb, :, cs]
        copy(ref, ref, ls.at[i], lr.at[i], d_c).wait_recv()
        pin[pb, zz, qs, x, :, cs] = (acc[lo * 2 + zz, qs, pb, :, cs] + lrx[zz, qs, pb, :, cs].astype(F32)).astype(BF)
        for r in (1, 2, 3):
            ref = pin.at[pb, zz, qs, x, :, cs]
            start(copy(ref, ref, ps.at[i, r - 1], pr.at[i, r - 1], d_x[r - 1]))

    def gathered(i, zz, q, *chunks):
        pb, cs = span_of(chunks)
        for r in (1, 2, 3):
            ref = pin.at[pb, zz, pl.ds(*q), (x + 4 - r) % 4, :, cs]
            copy(ref, ref, ps.at[i, r - 1], pr.at[i, r - 1], d_c).wait_recv()

    for cp in l_a:
        cp.wait()
    l_b.wait()
    for k in range(4):
        got(abuf.at[s_o, k, 1 - c], 7 + k)
    block(s_o, TOP, 0)
    block(s_o, LOW, 0)

    l_g.wait()
    got(gbuf.at[x, :, span(here_c, depth)], 11)
    got(gbuf.at[x, :, span(there, depth)], 0)
    got(gbuf.at[x, :, span(there_c, depth)], 1)
    for r in (1, 2, 3):
        start(copy(gbuf.at[x], gbuf.at[x], gs.at[r - 1], gr.at[r - 1], d_x[r - 1]))

    got(abuf.at[s_z, 2, c], 3)
    pass_on(abuf.at[s_z, 2, c], 20, d_c)
    got(abuf.at[s_z, 3, c], 6)
    pass_on(abuf.at[s_z, 3, c], 21, d_c)
    got(abuf.at[s_y, 0, c], 2)
    pass_on(abuf.at[s_y, 0, c], 22, d_c)
    got(abuf.at[s_z, 2, 1 - c], 20)
    got(abuf.at[s_z, 3, 1 - c], 21)
    block(s_z, LOW, 0)
    got(abuf.at[s_y, 1, c], 5)
    pass_on(abuf.at[s_y, 1, c], 23, d_c)
    got(abuf.at[s_y, 0, 1 - c], 22)
    got(abuf.at[s_y, 1, 1 - c], 23)
    block(s_y, TOP, 0)

    got(abuf.at[s_z, 0, c], 16)
    pass_on(abuf.at[s_y, 0, c], 28, d_z)
    pass_on(abuf.at[s_z, 0, c], 29, d_c)
    got(b_at(FIRST), 4)
    got(abuf.at[s_z, 1, c], 18)
    pass_on(abuf.at[s_y, 1, c], 30, d_z)
    pass_on(abuf.at[s_z, 1, c], 31, d_c)
    block(s_o, TOP, 1)
    block(s_y, TOP, 1)
    got(abuf.at[s_z, 0, 1 - c], 29)
    got(abuf.at[s_z, 1, 1 - c], 31)
    block(s_z, TOP, 0)
    block(s_o, LOW, 1)
    got(abuf.at[s_y, 2, c], 15)
    pass_on(abuf.at[s_y, 2, c], 33, d_c)

    third_z = copy(abuf.at[s_y, 2, c], abuf.at[s_y, 2, c], ss.at[32], rs.at[32], d_z)
    third_y = copy(abuf.at[s_z, 2, c], abuf.at[s_z, 2, c], ss.at[32], rs.at[32], d_y)
    pending.append(third_z)

    @pl.when(c == 0)
    def _():
        third_z.start()

    add_x(0, z0, TOP, 0)
    add_x(1, z0, TOP, 1)
    got(abuf.at[s_y, 3, c], 17)
    pass_on(abuf.at[s_y, 3, c], 35, d_c)
    block(s_z, TOP, 1)
    got(abuf.at[s_y, 2, 1 - c], 33)
    got(abuf.at[s_y, 3, 1 - c], 35)
    block(s_y, LOW, 0, 1)
    block(s_z, LOW, 1)

    h2 = depth // 2
    got(h_at(here, other_k), 12)
    send(hbuf.at[span(here * 2, h2), other_k], hbuf.at[span(here * 2, h2), own_k], 24, d_b)
    got(h_at(there, other_k), 13)
    send(hbuf.at[span(there * 2 + 1, h2), other_k], hbuf.at[span(there * 2 + 1, h2), own_k], 26, d_l)
    pass_on(h_at(here, other_k), 25, d_c)
    pass_on(h_at(there, other_k), 27, d_c)
    add_x(2, z0, LOW, 0)
    add_x(3, z0, LOW, 1)
    pass_on(abuf.at[s_z, 3, c], 34, d_y)
    add_y(0, z0, TOP, 0)
    add_y(1, z0, TOP, 1)

    got(hbuf.at[span(there * 2, h2), own_k], 24)
    got(hbuf.at[span(there * 2 + 1, h2), own_k], 26)
    pass_on(h_at(there, own_k), 36, d_c)
    l_h.wait()
    got(h_at(here_c, own_k), 14)
    got(h_at(here_c, other_k), 25)
    got(h_at(there_c, other_k), 27)
    for r in (1, 2, 3):
        src = (x + 4 - r) % 4
        copy(gbuf.at[src], gbuf.at[src], gs.at[r - 1], gr.at[r - 1], d_c).wait_recv()
    got(h_at(there_c, own_k), 36)
    part = jnp.dot(gbuf[...].reshape(2 * rows, 4 * depth), hbuf[...], preferred_element_type=F32)
    for k in (0, 1):
        cut = part[:, k * kg:][:, :kg].reshape(4, rows // 2, kg)
        zall[:, k] = cut
        zst[:, k] = cut.astype(zst.dtype)
    for r in (1, 2, 3):
        start(copy(zst.at[(z + r) % 4], zrx.at[r - 1], zs.at[r - 1], zr.at[r - 1], d_zs[r - 1]))
    add_y(2, z0, LOW, 0)
    add_y(3, z0, LOW, 1)

    got(b_at(REST), 19)

    @pl.loop(0, 3)
    def _(j):
        s = jnp.where(j == 0, s_o, jnp.where(j == 1, s_z, s_y))
        block(s, TOP, 2)
        block(s, LOW, 2)

    got(abuf.at[s_d, 0, c], 28)
    pass_on(abuf.at[s_d, 0, c], 37, d_c)
    got(abuf.at[s_d, 1, c], 30)
    pass_on(abuf.at[s_d, 1, c], 38, d_c)

    @pl.when(c == 1)
    def _():
        third_y.start()

    got(abuf.at[s_d, 0, 1 - c], 37)
    got(abuf.at[s_d, 1, 1 - c], 38)
    block(s_d, TOP, 0, 1, 2)
    add_x(4, z0, ALL, 2)

    mine, theirs = span(hi, 2), span(1 - hi, 2)
    for r in (1, 2, 3):
        copy(zst.at[0], zrx.at[r - 1], zs.at[r - 1], zr.at[r - 1], d_c).wait_recv()
    for k in (0, 1):
        total = zall[z, k] + zrx[0, k].astype(F32) + zrx[1, k].astype(F32) + zrx[2, k].astype(F32)
        pout[k, z0, mine, c] = total.astype(BF).reshape(2, qr, kg)
    pass_on(pout.at[:, z0, mine, c], 41, d_y)
    pass_on(pout.at[:, z0, mine, c], 45, d_z)
    pass_on(pout.at[:, z0, mine, c], 43, d_c)

    got(abuf.at[s_d, 3, c], 34)
    pass_on(abuf.at[s_d, 3, c], 40, d_c)
    got(abuf.at[s_d, 2, c], 32)
    pass_on(abuf.at[s_d, 2, c], 39, d_c)
    got(abuf.at[s_d, 3, 1 - c], 40)
    block(s_d, FOURTH, 0, 1, 2)
    add_x(5, 1 - z0, TOP, 1, 2)
    add_x(6, 1 - z0, TOP, 0)
    got(abuf.at[s_d, 2, 1 - c], 39)
    block(s_d, THIRD, 0, 1, 2)

    add_y(4, z0, ALL, 2)
    got(pout.at[:, z0, theirs, c], 41)
    pass_on(pout.at[:, z0, theirs, c], 42, d_z)
    pass_on(pout.at[:, z0, theirs, c], 46, d_c)
    add_y(5, 1 - z0, TOP, 1, 2)
    add_y(6, 1 - z0, TOP, 0)
    got(pout.at[:, 1 - z0, mine, c], 45)
    pass_on(pout.at[:, 1 - z0, mine, c], 44, d_c)
    add_x(7, 1 - z0, LOW, 1, 2)
    add_x(8, 1 - z0, LOW, 0)
    got(pout.at[:, 1 - z0, theirs, c], 42)
    pass_on(pout.at[:, 1 - z0, theirs, c], 47, d_c)
    add_y(7, 1 - z0, LOW, 1, 2)
    add_y(8, 1 - z0, LOW, 0)

    got(pout.at[:, z0, mine, 1 - c], 43)
    got(pout.at[:, z0, theirs, 1 - c], 46)
    got(pout.at[:, 1 - z0, mine, 1 - c], 44)
    got(pout.at[:, 1 - z0, theirs, 1 - c], 47)

    def squares(k, pb):
        left = pout[k].reshape(4 * rows, kg)
        right = pin[pb].reshape(4 * rows, kb)
        t = lax.dot_general(left, right, (((0,), (0,)), ((), ())), preferred_element_type=F32)
        return t * t

    hk = kg // 2
    upper, lower = pl.ds(0, hk), pl.ds(hk, hk)

    def e_copy(i, to):
        return copy(est.at[i], erx.at[i], es.at[i], er.at[i], to)

    def give(i, values, to):
        est[i] = values.astype(est.dtype)
        start(e_copy(i, to))

    def taken(i):
        e_copy(i, d_c).wait_recv()
        return erx[i].astype(F32)

    gathered(1, z0, TOP, 1)
    gathered(3, z0, LOW, 1)
    gathered(4, z0, ALL, 2)
    gathered(5, 1 - z0, TOP, 1, 2)
    gathered(7, 1 - z0, LOW, 1, 2)
    quad = squares(1, 1)
    give(0, quad[:hk], d_l)
    give(1, quad[hk:], d_q)
    quad = squares(0, 1)
    esum[0] = quad[:hk]
    give(2, quad[hk:], d_q)
    gathered(0, z0, TOP, 0)
    gathered(2, z0, LOW, 0)
    gathered(6, 1 - z0, TOP, 0)
    gathered(8, 1 - z0, LOW, 0)
    quad = squares(1, 0)
    esum[1] = quad[hk:]
    give(3, quad[:hk], d_l)
    give(4, esum[0] + taken(0), d_q)
    give(5, esum[1] + taken(1), d_l)
    total = squares(0, 0)
    out[lower] = total[hk:]
    out[upper] = total[:hk] + taken(3)
    out[lower] = out[lower] + taken(2)
    out[upper] = (out[upper] + taken(4)) * 0.25
    out[lower] = (out[lower] + taken(5)) * 0.25

    for cp in pending:
        cp.wait_send()

    @pl.loop(0, 4)
    def _(s):
        for m in (TOP, THIRD, FOURTH):
            for ch in range(3):
                for r in (1, 2, 3):
                    x_copy(s, m, ch, r).wait_send()


def per_device(acts, grads, basis_in, basis_out):
    rows, feats = acts.shape
    kb = basis_in.shape[1]
    depth, kg = basis_out.shape
    dma = pltpu.SemaphoreType.DMA
    return pl.pallas_call(
        kernel,
        out_shape=jax.ShapeDtypeStruct((kg, kb), F32),
        in_specs=[pl.BlockSpec(memory_space=pl.ANY)] * 4,
        out_specs=pl.BlockSpec(memory_space=pltpu.VMEM),
        scratch_shapes=[
            pltpu.VMEM((4, 4, 2, rows // 4, feats), BF),
            pltpu.VMEM((feats, 2 * kb), BF),
            pltpu.VMEM((4, rows // 2, 4 * depth), BF),
            pltpu.VMEM((4 * depth, 2 * kg), BF),
            pltpu.VMEM((2, 2, rows // 2, kb), F32),
            pltpu.VMEM((4, 4, 2, rows // 2, kb), BF),
            pltpu.VMEM((4, 4, 2, rows // 8, kb), F32),
            pltpu.VMEM((3, 4, 4, 2, rows // 8, kb), BF),
            pltpu.VMEM((2, 4, 2, rows // 8, kb), BF),
            pltpu.VMEM((2, 4, 2, rows // 8, kb), BF),
            pltpu.VMEM((2, 2, 4, 4, rows // 8, kb), BF),
            pltpu.VMEM((4, 2, rows // 2, kg), BF),
            pltpu.VMEM((4, 2, rows // 2, kg), F32),
            pltpu.VMEM((3, 2, rows // 2, kg), BF),
            pltpu.VMEM((2, 2, 4, 2, rows // 4, kg), BF),
            pltpu.VMEM((6, kg // 2, kb), BF),
            pltpu.VMEM((6, kg // 2, kb), BF),
            pltpu.VMEM((2, kg // 2, kb), F32),
            dma((7,)),
            dma((48,)), dma((48,)),
            dma((16, 3, 3)), dma((16, 3, 3)),
            dma((9,)), dma((9,)),
            dma((9, 3)), dma((9, 3)),
            dma((3,)), dma((3,)),
            dma((3,)), dma((3,)),
            dma((6,)), dma((6,)),
        ],
        compiler_params=pltpu.CompilerParams(
            collective_id=0, has_side_effects=True, vmem_limit_bytes=58 * 2**20
        ),
        cost_estimate=pl.CostEstimate(flops=14 * 10**9, bytes_accessed=7 * 10**6, transcendentals=0),
    )(acts, basis_in, grads, basis_out)


def solution(mesh):
    in_specs = (P("col", "row"), P("row", "col"), P("row", "col"), P("col", "row"))
    return jax.shard_map(
        per_device, mesh=mesh, in_specs=in_specs, out_specs=P("row", "col"), check_vma=False
    )
```

time: 449 us -> 122 us (0.27)
  blocking collectives: 272 us -> 0 us
  waiting for transfers between devices: 129 us -> 0 us
  Pallas kernels: 0 us -> 120 us
  matrix products: 32.9 us -> 0 us
  between operations: 13.4 us -> 0.01 us
    psum x2 -> x0, blocking collectives: 272 us -> none  [the longest x1 143 us: per_device(): proj_out = lax.psum(partial_out, 'col').astype(jnp.bfloat16)]
    all_gather x2 -> x0, waiting for transfers between devices: 128 us -> none  [the longest x1 72 us: per_device(): lax.all_gather(acts, 'col', axis=0, tiled=True)]
    pallas_call x0 -> x1, Pallas kernels: none -> 120 us  [per_device(): pl.pallas_call(kernel, out_shape=jax.ShapeDtypeStruct((kg, kb), F32), in_...]
    dot_general x3 -> x0, matrix products: 32.9 us -> none  [the longest x1 20.9 us: per_device(): jnp.dot(lax.all_gather(acts, 'col', axis=0, tiled=True), basis_in, prefer...]
  transfers between devices with their start and end apart: 2 -> 0, of which waited for: 2 -> 0; matrix products, arithmetic and copies ran while one was open for 2% -> 0% of each run, Pallas kernels for 0% -> 0%
where the time goes in v3:
time: 122 us
  Pallas kernels  120 us (98%)
  local copies, waits for them, and re-layouts  1.92 us (2%)
    pallas_call x1, Pallas kernels, per_device(): pl.pallas_call(kernel, out_shape=jax.ShapeDtypeStruct((kg, kb), F32), in_...  120 us

profile of v3, /device:TPU:0, one launch (start us, length us, event | category | flops | bytes accessed | tf_op | source)
XLA Modules:
  0.0 121.6 jit_solution(1459612750946193086)
XLA Ops:
  0.0 119.7 %shard_map.46 = f32[384,384]{1,0:T(8,128)} custom-call(bf16[256,3584]{1,0:T(8,128)(2,1)} %a.1, bf16[3584,384]{1,0:T(8,128)(2,1)} %b.1, bf16[512,512]{1,0:T(8,128)(2,1)} %g.1, bf16[512,384]{1,0:T(8,128)(2,1)} %h.1), custom_call_target="tpu_custom_call" | custom-call | flops 14000000000 | bytes 7000000 | tf_op jit(solution)/shard_map/pallas_call | solution.py:417
  119.7 1.9 %copy.6 = f32[384,384]{1,0:T(8,128)} copy(f32[384,384]{1,0:T(8,128)} %shard_map.46) | data formatting | bytes 1179648

commit v4 on v3

--- a/solution.py
+++ b/solution.py
@@ -12,6 +12,8 @@
 PIECES = (OWN, FIRST, REST)
 TOP, LOW, THIRD, FOURTH, ALL = (0, 2), (2, 2), (2, 1), (3, 1), (0, 4)
 MESSAGES = {TOP: [TOP], LOW: [THIRD, FOURTH], THIRD: [THIRD], FOURTH: [FOURTH], ALL: [TOP, THIRD, FOURTH]}
+NEAR = {(0, 0): 0, (0, 1): 1, (0, 2): 4, (2, 0): 2, (2, 1): 3, (2, 2): 4}
+FAR = {(0, 0): 6, (0, 1): 5, (0, 2): 5, (2, 0): 8, (2, 1): 7, (2, 2): 7}
 
 
 def kernel(
@@ -125,10 +127,12 @@
 
     def x_copy(s, q, ch, r):
         pb, c0, w = PIECES[ch]
-        u, qs, cs = s * 4 + q[0], pl.ds(*q), pl.ds(c0, w)
+        qs, cs = pl.ds(*q), pl.ds(c0, w)
+        key = (0 if q[0] == 0 else 2, ch)
+        piece = jnp.where(s % 2 == z0, NEAR[key], FAR[key])
         return copy(
             stg.at[s, qs, pb, span((x + r) % 4, xrows), cs], rx.at[r - 1, s, qs, pb, :, cs],
-            xs.at[u, ch, r - 1], xr.at[u, ch, r - 1], d_x[r - 1],
+            xs.at[0], xr.at[piece, s // 2], d_x[r - 1],
         )
 
     def block(s, q, *chunks):
@@ -159,11 +163,8 @@
         pb, cs = span_of(chunks)
         for hh in (1 - lo, lo):
             s = hh * 2 + zz
-            for m in MESSAGES[q]:
-                for ch in chunks:
-                    for r in range(3):
-                        ref = rx.at[r, s, pl.ds(*m), pb, :, pl.ds(*PIECES[ch][1:])]
-                        copy(ref, ref, xs.at[0, 0, 0], xr.at[s * 4 + m[0], ch, r], d_c).wait_recv()
+            ref = rx.at[:, s, qs, pb, :, cs]
+            copy(ref, ref, xs.at[0], xr.at[i, hh], d_c).wait_recv()
             total = acc[s, qs, pb, :, cs]
             for r in range(3):
                 total = total + rx[r, s, qs, pb, :, cs].astype(F32)
@@ -172,23 +173,22 @@
             else:
                 ref = lst.at[zz, qs, pb, :, cs]
                 ref[...] = total.astype(lst.dtype)
-                start(copy(ref, lrx.at[zz, qs, pb, :, cs], ls.at[i], lr.at[i], d_l))
+                copy(ref, lrx.at[zz, qs, pb, :, cs], ls.at[0], lr.at[i], d_l).start()
 
     def add_y(i, zz, q, *chunks):
         qs = pl.ds(*q)
         pb, cs = span_of(chunks)
         ref = lrx.at[zz, qs, pb, :, cs]
-        copy(ref, ref, ls.at[i], lr.at[i], d_c).wait_recv()
+        copy(ref, ref, ls.at[0], lr.at[i], d_c).wait_recv()
         pin[pb, zz, qs, x, :, cs] = (acc[lo * 2 + zz, qs, pb, :, cs] + lrx[zz, qs, pb, :, cs].astype(F32)).astype(BF)
         for r in (1, 2, 3):
             ref = pin.at[pb, zz, qs, x, :, cs]
-            start(copy(ref, ref, ps.at[i, r - 1], pr.at[i, r - 1], d_x[r - 1]))
+            copy(ref, ref, ps.at[0], pr.at[i], d_x[r - 1]).start()
 
     def gathered(i, zz, q, *chunks):
         pb, cs = span_of(chunks)
-        for r in (1, 2, 3):
-            ref = pin.at[pb, zz, pl.ds(*q), (x + 4 - r) % 4, :, cs]
-            copy(ref, ref, ps.at[i, r - 1], pr.at[i, r - 1], d_c).wait_recv()
+        ref = pin.at[pb, zz, pl.ds(*q), pl.ds(0, 3), :, cs]
+        copy(ref, ref, ps.at[0], pr.at[i], d_c).wait_recv()
 
     for cp in l_a:
         cp.wait()
@@ -401,12 +401,8 @@
     for cp in pending:
         cp.wait_send()
 
-    @pl.loop(0, 4)
-    def _(s):
-        for m in (TOP, THIRD, FOURTH):
-            for ch in range(3):
-                for r in (1, 2, 3):
-                    x_copy(s, m, ch, r).wait_send()
+    for ref, sem in ((stg.at[:, :, :, pl.ds(0, 3 * xrows)], xs), (lst, ls), (pin.at[:, :, :, pl.ds(0, 3)], ps)):
+        copy(ref, ref, sem.at[0], sem.at[0], d_c).wait_send()
 
 
 def per_device(acts, grads, basis_in, basis_out):
@@ -440,9 +436,9 @@
             pltpu.VMEM((2, kg // 2, kb), F32),
             dma((7,)),
             dma((48,)), dma((48,)),
-            dma((16, 3, 3)), dma((16, 3, 3)),
-            dma((9,)), dma((9,)),
-            dma((9, 3)), dma((9, 3)),
+            dma((1,)), dma((9, 2)),
+            dma((1,)), dma((9,)),
+            dma((1,)), dma((9,)),
             dma((3,)), dma((3,)),
             dma((3,)), dma((3,)),
             dma((6,)), dma((6,)),

time: 122 us -> 119 us (0.975)
  Pallas kernels: 120 us -> 117 us
    pallas_call x1, Pallas kernels: 120 us -> 117 us  [per_device(): pl.pallas_call(kernel, out_shape=jax.ShapeDtypeStruct((kg, kb), F32), in_...]
where the time goes in v4:
time: 119 us
  Pallas kernels  117 us (98%)
  local copies, waits for them, and re-layouts  1.92 us (2%)
    pallas_call x1, Pallas kernels, per_device(): pl.pallas_call(kernel, out_shape=jax.ShapeDtypeStruct((kg, kb), F32), in_...  117 us

profile of v4, /device:TPU:0, one launch (start us, length us, event | category | flops | bytes accessed | tf_op | source)
XLA Modules:
  0.0 118.5 jit_solution(15876923348693900729)
XLA Ops:
  0.0 116.6 %shard_map.46 = f32[384,384]{1,0:T(8,128)} custom-call(bf16[256,3584]{1,0:T(8,128)(2,1)} %a.1, bf16[3584,384]{1,0:T(8,128)(2,1)} %b.1, bf16[512,512]{1,0:T(8,128)(2,1)} %g.1, bf16[512,384]{1,0:T(8,128)(2,1)} %h.1), custom_call_target="tpu_custom_call" | custom-call | flops 14000000000 | bytes 7000000 | tf_op jit(solution)/shard_map/pallas_call | solution.py:413
  116.6 1.9 %copy.6 = f32[384,384]{1,0:T(8,128)} copy(f32[384,384]{1,0:T(8,128)} %shard_map.46) | data formatting | bytes 1179648

commit v5 on v4

--- a/solution.py
+++ b/solution.py
@@ -14,6 +14,10 @@
 MESSAGES = {TOP: [TOP], LOW: [THIRD, FOURTH], THIRD: [THIRD], FOURTH: [FOURTH], ALL: [TOP, THIRD, FOURTH]}
 NEAR = {(0, 0): 0, (0, 1): 1, (0, 2): 4, (2, 0): 2, (2, 1): 3, (2, 2): 4}
 FAR = {(0, 0): 6, (0, 1): 5, (0, 2): 5, (2, 0): 8, (2, 1): 7, (2, 2): 7}
+
+ACTS = (2, 3, 5, 6, 7, 8, 9, 10, 15, 16, 17, 18, 20, 21, 22, 23, 29, 31, 33, 35, 37, 38, 39, 40)
+HANDED = (28, 30, 32, 34)
+OTHERS = [i for i in range(48) if i not in ACTS + HANDED]
 
 
 def kernel(
@@ -59,13 +63,16 @@
         pending.append(cp)
 
     def send(src, dst, i, to):
-        start(copy(src, dst, ss.at[i], rs.at[i], to))
+        if i in OTHERS:
+            start(copy(src, dst, ss.at[2 + OTHERS.index(i)], rs.at[i], to))
+        else:
+            copy(src, dst, ss.at[int(i in HANDED)], rs.at[i], to).start()
 
     def pass_on(ref, i, to):
         send(ref, ref, i, to)
 
     def got(dst, i):
-        copy(dst, dst, ss.at[i], rs.at[i], d_c).wait_recv()
+        copy(dst, dst, ss.at[0], rs.at[i], d_c).wait_recv()
 
     def span(i, n):
         return pl.ds(pl.multiple_of(i * n, n), n)
@@ -203,7 +210,7 @@
     got(gbuf.at[x, :, span(there, depth)], 0)
     got(gbuf.at[x, :, span(there_c, depth)], 1)
     for r in (1, 2, 3):
-        start(copy(gbuf.at[x], gbuf.at[x], gs.at[r - 1], gr.at[r - 1], d_x[r - 1]))
+        copy(gbuf.at[x], gbuf.at[x], gs.at[0], gr.at[0], d_x[r - 1]).start()
 
     got(abuf.at[s_z, 2, c], 3)
     pass_on(abuf.at[s_z, 2, c], 20, d_c)
@@ -236,9 +243,8 @@
     got(abuf.at[s_y, 2, c], 15)
     pass_on(abuf.at[s_y, 2, c], 33, d_c)
 
-    third_z = copy(abuf.at[s_y, 2, c], abuf.at[s_y, 2, c], ss.at[32], rs.at[32], d_z)
-    third_y = copy(abuf.at[s_z, 2, c], abuf.at[s_z, 2, c], ss.at[32], rs.at[32], d_y)
-    pending.append(third_z)
+    third_z = copy(abuf.at[s_y, 2, c], abuf.at[s_y, 2, c], ss.at[1], rs.at[32], d_z)
+    third_y = copy(abuf.at[s_z, 2, c], abuf.at[s_z, 2, c], ss.at[1], rs.at[32], d_y)
 
     @pl.when(c == 0)
     def _():
@@ -274,9 +280,8 @@
     got(h_at(here_c, own_k), 14)
     got(h_at(here_c, other_k), 25)
     got(h_at(there_c, other_k), 27)
-    for r in (1, 2, 3):
-        src = (x + 4 - r) % 4
-        copy(gbuf.at[src], gbuf.at[src], gs.at[r - 1], gr.at[r - 1], d_c).wait_recv()
+    three = gbuf.at[pl.ds(0, 3)]
+    copy(three, three, gs.at[0], gr.at[0], d_c).wait_recv()
     got(h_at(there_c, own_k), 36)
     part = jnp.dot(gbuf[...].reshape(2 * rows, 4 * depth), hbuf[...], preferred_element_type=F32)
     for k in (0, 1):
@@ -284,7 +289,7 @@
         zall[:, k] = cut
         zst[:, k] = cut.astype(zst.dtype)
     for r in (1, 2, 3):
-        start(copy(zst.at[(z + r) % 4], zrx.at[r - 1], zs.at[r - 1], zr.at[r - 1], d_zs[r - 1]))
+        copy(zst.at[(z + r) % 4], zrx.at[r - 1], zs.at[0], zr.at[0], d_zs[r - 1]).start()
     add_y(2, z0, LOW, 0)
     add_y(3, z0, LOW, 1)
 
@@ -311,8 +316,7 @@
     add_x(4, z0, ALL, 2)
 
     mine, theirs = span(hi, 2), span(1 - hi, 2)
-    for r in (1, 2, 3):
-        copy(zst.at[0], zrx.at[r - 1], zs.at[r - 1], zr.at[r - 1], d_c).wait_recv()
+    copy(zrx, zrx, zs.at[0], zr.at[0], d_c).wait_recv()
     for k in (0, 1):
         total = zall[z, k] + zrx[0, k].astype(F32) + zrx[1, k].astype(F32) + zrx[2, k].astype(F32)
         pout[k, z0, mine, c] = total.astype(BF).reshape(2, qr, kg)
@@ -361,11 +365,11 @@
     upper, lower = pl.ds(0, hk), pl.ds(hk, hk)
 
     def e_copy(i, to):
-        return copy(est.at[i], erx.at[i], es.at[i], er.at[i], to)
+        return copy(est.at[i], erx.at[i], es.at[0], er.at[i], to)
 
     def give(i, values, to):
         est[i] = values.astype(est.dtype)
-        start(e_copy(i, to))
+        e_copy(i, to).start()
 
     def taken(i):
         e_copy(i, d_c).wait_recv()
@@ -401,7 +405,12 @@
     for cp in pending:
         cp.wait_send()
 
-    for ref, sem in ((stg.at[:, :, :, pl.ds(0, 3 * xrows)], xs), (lst, ls), (pin.at[:, :, :, pl.ds(0, 3)], ps)):
+    handed = abuf.at[0, pl.ds(0, 2)]
+    copy(handed, handed, ss.at[1], rs.at[32], d_c).wait_send()
+    sent = abuf.at[pl.ds(0, 3)]
+    copy(sent, sent, ss.at[0], rs.at[32], d_c).wait_send()
+
+    for ref, sem in ((stg.at[:, :, :, pl.ds(0, 3 * xrows)], xs), (lst, ls), (pin.at[:, :, :, pl.ds(0, 3)], ps), (three, gs), (zst.at[pl.ds(0, 3)], zs), (est, es)):
         copy(ref, ref, sem.at[0], sem.at[0], d_c).wait_send()
 
 
@@ -435,13 +444,13 @@
             pltpu.VMEM((6, kg // 2, kb), BF),
             pltpu.VMEM((2, kg // 2, kb), F32),
             dma((7,)),
-            dma((48,)), dma((48,)),
+            dma((2 + len(OTHERS),)), dma((48,)),
             dma((1,)), dma((9, 2)),
             dma((1,)), dma((9,)),
             dma((1,)), dma((9,)),
-            dma((3,)), dma((3,)),
-            dma((3,)), dma((3,)),
-            dma((6,)), dma((6,)),
+            dma((1,)), dma((1,)),
+            dma((1,)), dma((1,)),
+            dma((1,)), dma((6,)),
         ],
         compiler_params=pltpu.CompilerParams(
             collective_id=0, has_side_effects=True, vmem_limit_bytes=58 * 2**20

time: 119 us -> 118 us (level)
  no operation moved by 1% of the time
where the time goes in v5:
time: 118 us
  Pallas kernels  116 us (98%)
  local copies, waits for them, and re-layouts  1.92 us (2%)
    pallas_call x1, Pallas kernels, per_device(): pl.pallas_call(kernel, out_shape=jax.ShapeDtypeStruct((kg, kb), F32), in_...  116 us

profile of v5, /device:TPU:0, one launch (start us, length us, event | category | flops | bytes accessed | tf_op | source)
XLA Modules:
  0.0 118.1 jit_solution(5262691881675188329)
XLA Ops:
  0.0 116.2 %shard_map.46 = f32[384,384]{1,0:T(8,128)} custom-call(bf16[256,3584]{1,0:T(8,128)(2,1)} %a.1, bf16[3584,384]{1,0:T(8,128)(2,1)} %b.1, bf16[512,512]{1,0:T(8,128)(2,1)} %g.1, bf16[512,384]{1,0:T(8,128)(2,1)} %h.1), custom_call_target="tpu_custom_call" | custom-call | flops 14000000000 | bytes 7000000 | tf_op jit(solution)/shard_map/pallas_call | solution.py:422
  116.2 1.9 %copy.6 = f32[384,384]{1,0:T(8,128)} copy(f32[384,384]{1,0:T(8,128)} %shard_map.46) | data formatting | bytes 1179648
